TPU v7x, 32 devices: a whole 2x2x4 slice. The times are simulated.
32 devices in a mesh: groups: 2 (over y), seq: 4 (over z), dp: 2 (over x), sub: 2 (over core).
Axes of the slice: x: 2, y: 2, z: 4, core: 2. Of those that a mesh axis runs over, the one named last changes fastest.
Arguments:
- signal: bfloat16 [8, 2048, 512], P(('groups', 'dp', 'sub'), 'seq'), parts along dimension 0, may hold values from -6 to 6
- conv_weight: bfloat16 [512, 3, 1024], P(('dp', 'sub')), may hold values from -0.15625 to 0.15625
- proj_weight: bfloat16 [512, 512], P(('dp', 'sub')), may hold values from -0.25 to 0.25
- cotangent: bfloat16 [8, 2048, 512], P(('groups', 'dp', 'sub'), 'seq'), parts along dimension 0, may hold values from -6 to 6
Outputs:
- output: bfloat16 [8, 2048, 512], P(('groups', 'dp', 'sub'), 'seq'), parts along dimension 0
- grad_input: bfloat16 [8, 2048, 512], P(('groups', 'dp', 'sub'), 'seq'), parts along dimension 0
- grad_conv: float32 [1024, 3, 1024], P(('groups', 'dp', 'sub')), parts along dimension 0
- grad_proj: float32 [1024, 512], P(('groups', 'dp', 'sub')), parts along dimension 0
There are 2 independent parts, one for each index of `groups`. A program takes and returns all parts, laid end to end along the dimension named above; an argument that names none is the same for every part. Nothing has to cross between parts.
All inputs are finite; a program needn't handle non-finite values.
Results may differ from a plain program's by a relative error of at most 0.012.
Values may be sent and summed in bfloat16 or wider, within the bound.
A program may use at most 64 MiB of HBM per device.

v0:
```python
import math
import jax
import jax.numpy as jnp
from jax import lax
from jax.sharding import PartitionSpec as P

DILATION = 512


def passed_along(block, axis, distance):
    devices = range(lax.axis_size(axis))
    route = [(i - distance, i) for i in devices if i - distance in devices]
    return lax.ppermute(block, axis, route)


def relay_earlier(block, reach_blocks):
    blocks = [block]
    current = block
    for step_index in range(reach_blocks):
        current = passed_along(current, "seq", 1)
        blocks.append(current)
    return jnp.concatenate(blocks[::-1], axis=0)


def relay_later(block, reach_blocks):
    blocks = [block]
    current = block
    for step_index in range(reach_blocks):
        current = passed_along(current, "seq", -1)
        blocks.append(current)
    return jnp.concatenate(blocks, axis=0)


def local(signal, conv_weight, proj_weight, cotangent):
    signal_block = signal[0]
    upstream = cotangent[0]
    row_count, channels = signal_block.shape
    offsets = [tap_index * DILATION for tap_index in range(3)]
    reach_blocks = (2 * DILATION + row_count - 1) // row_count
    full_conv = lax.all_gather(conv_weight, ("dp", "sub"), axis=0, tiled=True)
    full_proj = lax.all_gather(proj_weight, ("dp", "sub"), axis=0, tiled=True)
    window = relay_earlier(signal_block, reach_blocks)
    base_row = reach_blocks * row_count
    taps = [window[base_row - offset : base_row - offset + row_count] for offset in offsets]
    preact = jnp.dot(taps[0], full_conv[:, 0, :], preferred_element_type=jnp.float32)
    for tap_index in range(1, 3):
        preact = preact + jnp.dot(
            taps[tap_index], full_conv[:, tap_index, :], preferred_element_type=jnp.float32
        )
    tanh_part = jnp.tanh(preact[:, :channels])
    gate_part = jax.nn.sigmoid(preact[:, channels:])
    gated = (tanh_part * gate_part).astype(jnp.bfloat16)
    output = (
        signal_block.astype(jnp.float32)
        + jnp.dot(gated, full_proj, preferred_element_type=jnp.float32)
    ).astype(jnp.bfloat16)
    transposed = (((1,), (1,)), ((), ()))
    grad_gated = lax.dot_general(
        upstream,
        lax.all_gather(proj_weight, ("dp", "sub"), axis=0, tiled=True),
        transposed,
        preferred_element_type=jnp.float32,
    )
    grad_pre = jnp.concatenate(
        [
            grad_gated * gate_part * (1.0 - tanh_part * tanh_part),
            grad_gated * tanh_part * gate_part * (1.0 - gate_part),
        ],
        axis=1,
    ).astype(jnp.bfloat16)
    ahead_window = relay_later(grad_pre, reach_blocks)
    futures = [ahead_window[offset : offset + row_count] for offset in offsets]
    panel = lax.all_gather(conv_weight, ("dp", "sub"), axis=0, tiled=True)
    summed = lax.dot_general(
        futures[0], panel[:, 0, :], transposed, preferred_element_type=jnp.float32
    )
    for tap_index in range(1, 3):
        summed = summed + lax.dot_general(
            futures[tap_index],
            panel[:, tap_index, :],
            transposed,
            preferred_element_type=jnp.float32,
        )
    grad_input = (upstream.astype(jnp.float32) + summed).astype(jnp.bfloat16)
    outer = (((0,), (0,)), ((), ()))
    terms = [
        lax.dot_general(taps[tap_index], grad_pre, outer, preferred_element_type=jnp.float32)
        for tap_index in range(3)
    ]
    conv_share = lax.psum_scatter(
        jnp.stack(terms, axis=1).astype(jnp.bfloat16),
        ("dp", "sub"),
        scatter_dimension=0,
        tiled=True,
    )
    proj_share = lax.psum_scatter(
        lax.dot_general(gated, upstream, outer, preferred_element_type=jnp.float32).astype(
            jnp.bfloat16
        ),
        ("dp", "sub"),
        scatter_dimension=0,
        tiled=True,
    )
    conv_total, proj_total = (
        lax.psum(conv_share, "seq").astype(jnp.float32),
        lax.psum(proj_share, "seq").astype(jnp.float32),
    )
    all_rows = row_count * lax.axis_size("seq") * lax.axis_size(("dp", "sub"))
    factor = 1.0 / math.sqrt(all_rows)
    return (output[None], grad_input[None], conv_total * factor, proj_total * factor)


def solution(mesh):
    placed = (
        P(("groups", "dp", "sub"), "seq", None),
        P(("dp", "sub"), None, None),
        P(("dp", "sub"), None),
        P(("groups", "dp", "sub"), "seq", None),
    )
    return jax.shard_map(
        local,
        mesh=mesh,
        in_specs=placed,
        out_specs=(
            P(("groups", "dp", "sub"), "seq", None),
            P(("groups", "dp", "sub"), "seq", None),
            P(("groups", "dp", "sub"), None, None),
            P(("groups", "dp", "sub"), None),
        ),
        check_vma=False,
    )
```

profile of v0, /device:TPU:0, one launch (start us, length us, event | category | flops | bytes accessed | tf_op | source)
XLA Modules:
  0.0 176.0 jit_solution(7137187538387217942)
XLA Ops:
  7.2 0.0 all-gather.2.cloned.1.call-start
  7.2 0.7 all-gather.2.cloned.1.call-update
  7.9 0.0 reduce-scatter.7.cloned.1.call-start
  7.9 5.0 %collective-permute-start = (bf16[512,512]{1,0:T(8,128)(2,1)}, bf16[512,512]{1,0:T(8,128)(2,1)S(1)}, u32[]{:S(2)}, u32[]{:S(2)}) collective-permute-start(bf16[512,512]{1,0:T(8,128)(2,1)} %bitcast.57), channel_id=1, source_target_pairs={{0,4},{4,8},{8,12},{1,5},{5,9},{9,13},{2,6},{6,10},{10,14},{3,7},{... | collective-permute-start | bytes 1572872 | tf_op jit(solution)/shard_map/ppermute | solution.py:13
  12.9 7.4 %all_gather.9 = bf16[512,512]{1,0:T(8,128)(2,1)S(1)} all-gather(bf16[128,512]{1,0:T(8,128)(2,1)} %param.6), channel_id=1, replica_groups=mesh['groups'=2,'seq'=4,'dp'=2,'sub'=2] {'dp','sub'}, dimensions={0}, use_global_device_ids=true | all-gather | bytes 655360 | tf_op jit(solution)/shard_map/all_gather | solution.py:41
  20.3 4.1 %collective-permute-done = bf16[512,512]{1,0:T(8,128)(2,1)S(1)} collective-permute-done((bf16[512,512]{1,0:T(8,128)(2,1)}, bf16[512,512]{1,0:T(8,128)(2,1)S(1)}, u32[]{:S(2)}, u32[]{:S(2)}) %collective-permute-start) | collective-permute-done | bytes 524320 | tf_op jit(solution)/shard_map/ppermute | solution.py:13
  24.4 4.3 %collective-permute-start.1 = (bf16[512,512]{1,0:T(8,128)(2,1)S(1)}, bf16[512,512]{1,0:T(8,128)(2,1)S(1)}, u32[]{:S(2)}, u32[]{:S(2)}) collective-permute-start(bf16[512,512]{1,0:T(8,128)(2,1)S(1)} %collective-permute-done), channel_id=1, source_target_pairs={{0,4},{4,8},{8,12},{1,5},{5,9},{9,13},{2,6},{6,10},{10,14},{3,7},{... | collective-permute-start | bytes 1572872 | tf_op jit(solution)/shard_map/ppermute | solution.py:13
  28.7 12.2 %all-gather.2.cloned.1.call-done = bf16[512,3,1024]{2,0,1:T(8,128)(2,1)} async-done(((bf16[128,3,1024]{2,0,1:T(8,128)(2,1)}), bf16[512,3,1024]{2,0,1:T(8,128)(2,1)}) %all-gather.2.cloned.1.call-update) | async-done | bytes 3145744 | tf_op jit(solution)/shard_map/all_gather | solution.py:40
  40.8 2.2 %fusion.12 = f32[512,1024]{1,0:T(8,128)S(1)} fusion(bf16[512,3,1024]{2,0,1:T(8,128)(2,1)} %all-gather.2.cloned.1.call-done, bf16[1,512,512]{2,1,0:T(8,128)(2,1)} %param.4), kind=kOutput, calls=%fused_computation.31 | convolution fusion | flops 536870912 | bytes 3670016 | tf_op jit(solution)/shard_map/dot_general | solution.py:45
  43.1 0.1 copy-done
  43.2 0.7 fusion.13
  43.9 0.0 copy-start.10
  43.9 0.0 collective-permute-done.1
  44.0 0.8 add_add_fusion
  44.7 0.2 copy-done.10
  45.0 1.7 multiply_convert_fusion.1
  46.7 0.7 fusion.1
  47.4 0.7 fusion.3
  48.2 0.7 fusion.2
  49.0 0.3 pad_maximum_fusion
  49.3 3.1 %copy.17 = bf16[512,3072]{1,0:T(8,128)(2,1)} copy(bf16[512,3072]{0,1:T(8,128)(2,1)S(1)} %bitcast.55) | data formatting | bytes 6291456
  52.4 0.0 reduce-scatter.7.cloned.1.call-update
  52.4 0.0 reduce-scatter.5.cloned.1.call-start
  52.4 1.0 copy-done.5
  53.4 0.2 copy-done.7
  53.6 1.1 pad_maximum_fusion.1
  54.7 1.3 collective-permute-start.2
  56.0 0.0 copy-done.8
  56.0 0.0 copy-done.11
  56.0 1.3 convolution_convert_fusion.3
  57.3 0.0 reduce-scatter.5.cloned.1.call-update
  57.3 0.0 all-reduce.3.cloned.1.call-start
  57.3 24.9 %collective-permute-done.2 = bf16[512,1024]{1,0:T(8,128)(2,1)} collective-permute-done((bf16[512,1024]{1,0:T(8,128)(2,1)}, bf16[512,1024]{1,0:T(8,128)(2,1)}, u32[]{:S(2)}, u32[]{:S(2)}) %collective-permute-start.2) | collective-permute-done | bytes 1048608 | tf_op jit(solution)/shard_map/ppermute | solution.py:13
  82.2 1.3 collective-permute-start.3
  83.5 2.6 %fusion.7 = bf16[1,512,512]{2,1,0:T(8,128)(2,1)} fusion(bf16[512,512]{1,0:T(8,128)(2,1)} %get-tuple-element.16, bf16[512,512]{1,0:T(8,128)(2,1)} %copy-done.3, bf16[1,512,512]{2,1,0:T(8,128)(2,1)} %param.4), kind=kOutput, calls=%fused_computation.17 | convolution fusion | flops 269221888 | bytes 2097152 | tf_op jit(solution)/shard_map/dot_general | solution.py:55
  86.1 4.4 %reduce-scatter.7.cloned.1.call-done = bf16[128,3072]{1,0:T(8,128)(2,1)} async-done(((bf16[512,3072]{1,0:T(8,128)(2,1)}), bf16[128,3072]{1,0:T(8,128)(2,1)}) %reduce-scatter.7.cloned.1.call-update) | async-done | bytes 786448
  90.5 2.3 %copy.18 = bf16[128,3072]{0,1:T(8,128)(2,1)} copy(bf16[128,3072]{1,0:T(8,128)(2,1)} %reduce-scatter.7.cloned.1.call-done) | data formatting | bytes 1572864
  92.8 22.1 %reduce-scatter.5.cloned.1.call-done = bf16[128,512]{1,0:T(8,128)(2,1)} async-done(((bf16[512,512]{1,0:T(8,128)(2,1)}), bf16[128,512]{1,0:T(8,128)(2,1)}) %reduce-scatter.5.cloned.1.call-update) | async-done | bytes 131088 | tf_op jit(solution)/shard_map/reduce_scatter | solution.py:96
  114.9 0.0 all-reduce.3.cloned.1.call-update
  114.9 1.9 %fusion.11 = f32[512,512]{1,0:T(8,128)S(1)} fusion(bf16[512,3,1024]{2,0,1:T(8,128)(2,1)S(1)} %copy-done.1, bf16[512,512]{1,0:T(8,128)(2,1)} %copy-done.6, bf16[512,512]{1,0:T(8,128)(2,1)} %copy-done.4), kind=kOutput, calls=%fused_computation.30 | convolution fusion | flops 538968064 | bytes 3145728 | tf_op jit(solution)/shard_map/dot_general | solution.py:74
  116.8 0.0 copy-start.12
  116.9 2.0 %convolution_add_fusion.1 = f32[512,512]{1,0:T(8,128)S(1)} fusion(f32[512,512]{1,0:T(8,128)S(1)} %fusion.11, bf16[512,1024]{1,0:T(8,128)(2,1)} %collective-permute-done.2, bf16[512,3,1024]{2,0,1:T(8,128)(2,1)S(1)} %copy-done.1), kind=kOutput, calls=%fused_computation.8 | convolution fusion | flops 537133056 | bytes 4194304 | tf_op jit(solution)/shard_map/dot_general | solution.py:78
  118.9 0.0 collective-permute-done.3
  118.9 2.8 %fusion.6 = bf16[1,512,512]{2,1,0:T(8,128)(2,1)} fusion(f32[512,512]{1,0:T(8,128)S(1)} %convolution_add_fusion.1, bf16[512,1024]{1,0:T(8,128)(2,1)} %collective-permute-done.3, bf16[512,3,1024]{2,0,1:T(8,128)(2,1)S(1)} %copy-done.1, bf16[1,512,512]{2,1,0:T(8,128)(2,1)S(1)} %copy-done.12), kind=kOutput, calls=%fused_computation.16 | convolution fusion | flops 537919488 | bytes 4194304 | tf_op jit(solution)/shard_map/dot_general | solution.py:78
  121.7 44.2 %all-reduce.3.cloned.1.call-done = (bf16[128,3,1024]{0,2,1:T(8,128)(2,1)}, bf16[128,512]{1,0:T(8,128)(2,1)}) async-done(((bf16[128,3,1024]{0,2,1:T(8,128)(2,1)}, bf16[128,512]{1,0:T(8,128)(2,1)}), (bf16[128,3,1024]{0,2,1:T(8,128)(2,1)}, bf16[128,512]{1,0:T(8,128)(2,1)})) %all-reduce.3.cloned.1.call-update) | async-done | bytes 917520 | tf_op jit(solution)/shard_map/psum | solution.py:105
  165.9 1.3 convert_multiply_fusion
  167.2 1.6 copy.13
  168.8 0.7 convert_multiply_fusion.1
  (18 shorter events, 0.0 us)
Async XLA Ops:
  7.2 33.7 %all-gather.2.cloned.1.call-start = ((), (), s32[]{:S(2)}) async-start(), calls=%async_computation.2 | async-start | bytes 3932160 | tf_op jit(solution)/shard_map/all_gather | solution.py:40
  7.9 82.6 %reduce-scatter.7.cloned.1.call-start = ((), (), s32[]{:S(2)}) async-start(), calls=%async_computation.4 | async-start | bytes 3932160
  7.9 16.4 %collective-permute-start = (bf16[512,512]{1,0:T(8,128)(2,1)}, bf16[512,512]{1,0:T(8,128)(2,1)S(1)}, u32[]{:S(2)}, u32[]{:S(2)}) collective-permute-start(bf16[512,512]{1,0:T(8,128)(2,1)} %bitcast.57), channel_id=1, source_target_pairs={{0,4},{4,8},{8,12},{1,5},{5,9},{9,13},{2,6},{6,10},{10,14},{3,7},{... | collective-permute-start | bytes 1572872 | tf_op jit(solution)/shard_map/ppermute | solution.py:13
  20.3 24.4 %copy-start.3 = (bf16[512,512]{1,0:T(8,128)(2,1)}, bf16[512,512]{1,0:T(8,128)(2,1)S(1)}, u32[]{:S(2)}) copy-start(bf16[512,512]{1,0:T(8,128)(2,1)S(1)} %all_gather.9) | copy-start | bytes 1572868
  24.4 19.6 %collective-permute-start.1 = (bf16[512,512]{1,0:T(8,128)(2,1)S(1)}, bf16[512,512]{1,0:T(8,128)(2,1)S(1)}, u32[]{:S(2)}, u32[]{:S(2)}) collective-permute-start(bf16[512,512]{1,0:T(8,128)(2,1)S(1)} %collective-permute-done), channel_id=1, source_target_pairs={{0,4},{4,8},{8,12},{1,5},{5,9},{9,13},{2,6},{6,10},{10,14},{3,7},{... | collective-permute-start | bytes 1572872 | tf_op jit(solution)/shard_map/ppermute | solution.py:13
  40.8 2.4 %copy-start = (bf16[512,3,1024]{2,0,1:T(8,128)(2,1)S(1)}, bf16[512,3,1024]{2,0,1:T(8,128)(2,1)}, u32[]{:S(2)}) copy-start(bf16[512,3,1024]{2,0,1:T(8,128)(2,1)} %all-gather.2.cloned.1.call-done) | copy-start | bytes 9437188
  43.9 1.0 copy-start.10
  45.0 1.7 copy-start.2
  46.7 1.5 copy-start.4
  46.7 1.5 copy-start.6
  52.4 1.0 copy-start.5
  52.4 1.2 copy-start.7
  52.4 3.6 %copy-start.8 = (bf16[512,512]{1,0:T(8,128)(2,1)S(1)}, bf16[512,512]{1,0:T(8,128)(2,1)}, u32[]{:S(2)}) copy-start(bf16[512,512]{1,0:T(8,128)(2,1)} %get-tuple-element.16) | copy-start | bytes 1572868
  52.4 3.6 %copy-start.11 = (bf16[1,512,512]{2,1,0:T(8,128)(2,1)S(1)}, bf16[1,512,512]{2,1,0:T(8,128)(2,1)}, u32[]{:S(2)}) copy-start(bf16[1,512,512]{2,1,0:T(8,128)(2,1)} %param.7) | copy-start | bytes 1572868
  52.4 62.5 %reduce-scatter.5.cloned.1.call-start = ((), (), s32[]{:S(2)}) async-start(), calls=%async_computation.3 | async-start | bytes 655360 | tf_op jit(solution)/shard_map/reduce_scatter | solution.py:96
  54.7 27.5 %collective-permute-start.2 = (bf16[512,1024]{1,0:T(8,128)(2,1)}, bf16[512,1024]{1,0:T(8,128)(2,1)}, u32[]{:S(2)}, u32[]{:S(2)}) collective-permute-start(bf16[512,1024]{1,0:T(8,128)(2,1)} %pad_maximum_fusion.1), channel_id=1, source_target_pairs={{4,0},{8,4},{12,8},{5,1},{9,5},{13,9},{6,2},{10,6},{14,10},{7,3},{... | collective-permute-start | bytes 3145736 | tf_op jit(solution)/shard_map/ppermute | solution.py:13
  57.3 57.6 %copy-start.1 = (bf16[512,3,1024]{2,0,1:T(8,128)(2,1)S(1)}, bf16[512,3,1024]{2,0,1:T(8,128)(2,1)}, u32[]{:S(2)}) copy-start(bf16[512,3,1024]{2,0,1:T(8,128)(2,1)} %all-gather.2.cloned.1.call-done) | copy-start | bytes 9437188
  57.3 108.6 %all-reduce.3.cloned.1.call-start = ((), (), s32[]{:S(2)}) async-start(), calls=%async_computation.5 | async-start | bytes 1835008 | tf_op jit(solution)/shard_map/psum | solution.py:105
  82.2 36.7 %collective-permute-start.3 = (bf16[512,1024]{1,0:T(8,128)(2,1)}, bf16[512,1024]{1,0:T(8,128)(2,1)}, u32[]{:S(2)}, u32[]{:S(2)}) collective-permute-start(bf16[512,1024]{1,0:T(8,128)(2,1)} %collective-permute-done.2), channel_id=1, source_target_pairs={{4,0},{8,4},{12,8},{5,1},{9,5},{13,9},{6,2},{10,6},{14,10},{7,3},{... | collective-permute-start | bytes 3145736 | tf_op jit(solution)/shard_map/ppermute | solution.py:13
  116.8 2.1 %copy-start.12 = (bf16[1,512,512]{2,1,0:T(8,128)(2,1)S(1)}, bf16[1,512,512]{2,1,0:T(8,128)(2,1)}, u32[]{:S(2)}) copy-start(bf16[1,512,512]{2,1,0:T(8,128)(2,1)} %param.7) | copy-start | bytes 1572868
  167.2 1.6 copy-start.9
Sparse Core Ops, SparseCore 0:
  9.6 31.2 all-gather.1
  52.5 37.9 reduce-scatter.6
  93.2 21.6 reduce-scatter.4
  117.7 48.1 all-reduce.2
where the time goes:
time: 177 us; the launch traced here: 176 us
  waiting for transfers between devices  113 us (64%)
  matrix products  18.3 us (10%)
  between operations  14 us (8%)
  starting transfers between devices  12 us (7%)
  local copies, waits for them, and re-layouts  8.45 us (5%)
  blocking collectives  7.38 us (4%)
  other arithmetic  3.45 us (2%)
    psum x1, waiting for transfers between devices, local(): lax.psum(conv_share, 'seq').astype(jnp.float32)  44.2 us
    ppermute x4, waiting for transfers between devices, passed_along(): return lax.ppermute(block, axis, route)  28.9 us
    reduce_scatter x1, waiting for transfers between devices, local(): lax.psum_scatter(lax.dot_general(gated, upstream, outer, preferred_elemen...  22.1 us
    all_gather x1, waiting for transfers between devices, local(): full_conv = lax.all_gather(conv_weight, ('dp', 'sub'), axis=0, tiled=True)  12.2 us
    ppermute x4, starting transfers between devices, passed_along(): return lax.ppermute(block, axis, route)  11.8 us
    unnamed x29, local copies, waits for them, and re-layouts  8.45 us
    all_gather x1, blocking collectives, local(): full_proj = lax.all_gather(proj_weight, ('dp', 'sub'), axis=0, tiled=True)  7.38 us
    unnamed x5, waiting for transfers between devices  5.17 us
  transfers between devices with their start and end apart: 8, of which 6 were waited for; matrix products, arithmetic and copies ran while one was open for 10% of the time, Pallas kernels for 0%

commit v1 on v0

--- a/solution.py
+++ b/solution.py
@@ -3,6 +3,7 @@
 import jax.numpy as jnp
 from jax import lax
 from jax.sharding import PartitionSpec as P
+from jax.lax import all_gather
 
 DILATION = 512
 
@@ -101,8 +102,13 @@
         scatter_dimension=0,
         tiled=True,
     )
+
+    def arrange_pages(x0, along_axis="seq"):
+        z_new = jnp.sum(all_gather(x0, along_axis), axis=0)
+        return z_new
+
     conv_total, proj_total = (
-        lax.psum(conv_share, "seq").astype(jnp.float32),
+        arrange_pages(conv_share).astype(jnp.float32),
         lax.psum(proj_share, "seq").astype(jnp.float32),
     )
     all_rows = row_count * lax.axis_size("seq") * lax.axis_size(("dp", "sub"))

time: 177 us -> 243 us (1.37)
  waiting for transfers between devices: 113 us -> 169 us
  other arithmetic: 3.45 us -> 9.86 us
  local copies, waits for them, and re-layouts: 8.45 us -> 12 us
    psum x1, waiting for transfers between devices: 44.2 us -> 0.01 us  [local(): lax.psum(proj_share, 'seq').astype(jnp.float32)]
    ppermute x4, waiting for transfers between devices: 28.9 us -> 71.9 us  [passed_along(): return lax.ppermute(block, axis, route)]
    unnamed x5 -> x6, waiting for transfers between devices: 5.17 us -> 41.4 us
    all_gather x0 -> x1, waiting for transfers between devices: none -> 27.7 us  [arrange_pages(): z_new = jnp.sum(all_gather(x0, along_axis), axis=0)]
    reduce_scatter x1, waiting for transfers between devices: 22.1 us -> 16 us  [local(): lax.psum_scatter(lax.dot_general(gated, upstream, outer, preferred_elemen...]
    reduce_sum x0 -> x1, other arithmetic: none -> 5.18 us  [arrange_pages(): z_new = jnp.sum(all_gather(x0, along_axis), axis=0)]
    all_gather x0 -> x1, local copies, waits for them, and re-layouts: none -> 3.75 us  [arrange_pages(): z_new = jnp.sum(all_gather(x0, along_axis), axis=0)]
    unnamed x29 -> x23, local copies, waits for them, and re-layouts: 8.45 us -> 8.2 us
  transfers between devices with their start and end apart: 8 -> 9, of which waited for: 6 -> 7; matrix products, arithmetic and copies ran while one was open for 10% -> 10% of each run, Pallas kernels for 0% -> 0%
where the time goes in v1:
time: 243 us; the launch traced here: 242 us
  waiting for transfers between devices  169 us (70%)
  matrix products  17.6 us (7%)
  between operations  14 us (6%)
  starting transfers between devices  12.3 us (5%)
  local copies, waits for them, and re-layouts  12 us (5%)
  other arithmetic  9.86 us (4%)
  blocking collectives  7.38 us (3%)
    ppermute x4, waiting for transfers between devices, passed_along(): return lax.ppermute(block, axis, route)  71.9 us
    unnamed x6, waiting for transfers between devices  41.4 us
    all_gather x1, waiting for transfers between devices, arrange_pages(): z_new = jnp.sum(all_gather(x0, along_axis), axis=0)  27.7 us
    reduce_scatter x1, waiting for transfers between devices, local(): lax.psum_scatter(lax.dot_general(gated, upstream, outer, preferred_elemen...  16 us
    all_gather x1, waiting for transfers between devices, local(): full_conv = lax.all_gather(conv_weight, ('dp', 'sub'), axis=0, tiled=True)  12.2 us
    ppermute x4, starting transfers between devices, passed_along(): return lax.ppermute(block, axis, route)  12.1 us
    unnamed x23, local copies, waits for them, and re-layouts  8.2 us
    all_gather x1, blocking collectives, local(): full_proj = lax.all_gather(proj_weight, ('dp', 'sub'), axis=0, tiled=True)  7.38 us
  transfers between devices with their start and end apart: 9, of which 7 were waited for; matrix products, arithmetic and copies ran while one was open for 10% of the time, Pallas kernels for 0%

profile of v1, /device:TPU:0, one launch (start us, length us, event | category | flops | bytes accessed | tf_op | source)
XLA Modules:
  0.0 242.3 jit_solution(13397818497920763570)
XLA Ops:
  7.2 0.0 all-gather.4.cloned.1.call-start
  7.2 0.7 all-gather.4.cloned.1.call-update
  7.9 0.0 reduce-scatter.5.cloned.1.call-start
  7.9 5.0 %collective-permute-start = (bf16[512,512]{1,0:T(8,128)(2,1)}, bf16[512,512]{1,0:T(8,128)(2,1)S(1)}, u32[]{:S(2)}, u32[]{:S(2)}) collective-permute-start(bf16[512,512]{1,0:T(8,128)(2,1)} %bitcast.59), channel_id=1, source_target_pairs={{0,4},{4,8},{8,12},{1,5},{5,9},{9,13},{2,6},{6,10},{10,14},{3,7},{... | collective-permute-start | bytes 1572872 | tf_op jit(solution)/shard_map/ppermute | solution.py:14
  12.9 7.4 %all_gather.15 = bf16[512,512]{1,0:T(8,128)(2,1)S(1)} all-gather(bf16[128,512]{1,0:T(8,128)(2,1)} %param.6), channel_id=1, replica_groups=mesh['groups'=2,'seq'=4,'dp'=2,'sub'=2] {'dp','sub'}, dimensions={0}, use_global_device_ids=true | all-gather | bytes 655360 | tf_op jit(solution)/shard_map/all_gather | solution.py:42
  20.3 4.1 %collective-permute-done = bf16[512,512]{1,0:T(8,128)(2,1)S(1)} collective-permute-done((bf16[512,512]{1,0:T(8,128)(2,1)}, bf16[512,512]{1,0:T(8,128)(2,1)S(1)}, u32[]{:S(2)}, u32[]{:S(2)}) %collective-permute-start) | collective-permute-done | bytes 524320 | tf_op jit(solution)/shard_map/ppermute | solution.py:14
  24.4 4.3 %collective-permute-start.1 = (bf16[512,512]{1,0:T(8,128)(2,1)S(1)}, bf16[512,512]{1,0:T(8,128)(2,1)S(1)}, u32[]{:S(2)}, u32[]{:S(2)}) collective-permute-start(bf16[512,512]{1,0:T(8,128)(2,1)S(1)} %collective-permute-done), channel_id=1, source_target_pairs={{0,4},{4,8},{8,12},{1,5},{5,9},{9,13},{2,6},{6,10},{10,14},{3,7},{... | collective-permute-start | bytes 1572872 | tf_op jit(solution)/shard_map/ppermute | solution.py:14
  28.7 12.2 %all-gather.4.cloned.1.call-done = bf16[512,3,1024]{2,0,1:T(8,128)(2,1)} async-done(((bf16[128,3,1024]{2,0,1:T(8,128)(2,1)}), bf16[512,3,1024]{2,0,1:T(8,128)(2,1)}) %all-gather.4.cloned.1.call-update) | async-done | bytes 3145744 | tf_op jit(solution)/shard_map/all_gather | solution.py:41
  40.8 2.2 fusion.12
  43.1 0.1 copy-done
  43.2 0.7 fusion.13
  43.9 0.0 copy-start.9
  43.9 0.8 add_add_fusion
  44.7 0.2 copy-done.9
  45.0 0.9 multiply_convert_fusion.1
  45.9 0.0 copy-start.8
  45.9 0.8 copy-done.8
  46.7 1.3 convolution_convert_fusion.3
  47.9 0.0 reduce-scatter.5.cloned.1.call-update
  48.0 0.0 reduce-scatter.7.cloned.1.call-start
  48.0 0.7 fusion.1
  48.8 0.7 fusion.3
  49.5 0.7 fusion.2
  50.3 0.3 pad_maximum_fusion
  50.6 3.1 %copy.16 = bf16[512,3072]{1,0:T(8,128)(2,1)} copy(bf16[512,3072]{0,1:T(8,128)(2,1)S(1)} %bitcast.57) | data formatting | bytes 6291456
  53.7 0.0 reduce-scatter.7.cloned.1.call-update
  53.7 0.0 all-reduce.2.cloned.1.call-start
  53.8 16.0 %reduce-scatter.5.cloned.1.call-done = bf16[128,512]{1,0:T(8,128)(2,1)} async-done(((bf16[512,512]{1,0:T(8,128)(2,1)}), bf16[128,512]{1,0:T(8,128)(2,1)}) %reduce-scatter.5.cloned.1.call-update) | async-done | bytes 131088 | tf_op jit(solution)/shard_map/reduce_scatter | solution.py:97
  69.8 0.0 all-reduce.2.cloned.1.call-update
  69.8 0.0 all-gather.6.cloned.1.call-start
  69.8 40.6 %reduce-scatter.7.cloned.1.call-done = bf16[128,3072]{1,0:T(8,128)(2,1)} async-done(((bf16[512,3072]{1,0:T(8,128)(2,1)}), bf16[128,3072]{1,0:T(8,128)(2,1)}) %reduce-scatter.7.cloned.1.call-update) | async-done | bytes 786448
  110.4 2.4 copy.17
  112.8 0.0 all-gather.6.cloned.1.call-update
  112.9 1.4 pad_maximum_fusion.1
  114.3 1.4 collective-permute-start.2
  115.8 29.4 %collective-permute-done.2 = bf16[512,1024]{1,0:T(8,128)(2,1)} collective-permute-done((bf16[512,1024]{1,0:T(8,128)(2,1)S(1)}, bf16[512,1024]{1,0:T(8,128)(2,1)}, u32[]{:S(2)}, u32[]{:S(2)}) %collective-permute-start.2) | collective-permute-done | bytes 1048608 | tf_op jit(solution)/shard_map/ppermute | solution.py:14
  145.1 1.5 collective-permute-start.3
  146.6 2.6 %fusion.7 = bf16[1,512,512]{2,1,0:T(8,128)(2,1)} fusion(bf16[512,512]{1,0:T(8,128)(2,1)} %copy-done.8, bf16[512,512]{1,0:T(8,128)(2,1)} %copy-done.3, bf16[1,512,512]{2,1,0:T(8,128)(2,1)} %param.4), kind=kOutput, calls=%fused_computation.17 | convolution fusion | flops 269221888 | bytes 2097152 | tf_op jit(solution)/shard_map/dot_general | solution.py:56
  149.2 0.8 fusion.11
  150.0 2.9 %convolution_add_fusion.1 = f32[512,512]{1,0:T(8,128)} fusion(f32[512,512]{1,0:T(8,128)S(1)} %fusion.11, bf16[512,1024]{1,0:T(8,128)(2,1)} %collective-permute-done.2, bf16[512,3,1024]{2,0,1:T(8,128)(2,1)S(1)} %copy-done.1), kind=kOutput, calls=%fused_computation.8 | convolution fusion | flops 537133056 | bytes 4194304 | tf_op jit(solution)/shard_map/dot_general | solution.py:79
  152.9 1.6 convert_multiply_fusion.1
  154.6 38.4 %collective-permute-done.3 = bf16[512,1024]{1,0:T(8,128)(2,1)} collective-permute-done((bf16[512,1024]{1,0:T(8,128)(2,1)}, bf16[512,1024]{1,0:T(8,128)(2,1)}, u32[]{:S(2)}, u32[]{:S(2)}) %collective-permute-start.3) | collective-permute-done | bytes 1048608 | tf_op jit(solution)/shard_map/ppermute | solution.py:14
  193.0 3.2 %fusion.6 = bf16[1,512,512]{2,1,0:T(8,128)(2,1)} fusion(f32[512,512]{1,0:T(8,128)} %convolution_add_fusion.1, bf16[512,1024]{1,0:T(8,128)(2,1)} %collective-permute-done.3, bf16[512,3,1024]{2,0,1:T(8,128)(2,1)S(1)} %copy-done.1, bf16[1,512,512]{2,1,0:T(8,128)(2,1)} %param.7), kind=kOutput, calls=%fused_computation.16 | convolution fusion | flops 537919488 | bytes 4194304 | tf_op jit(solution)/shard_map/dot_general | solution.py:79
  196.2 27.7 %all-gather.6.cloned.1.call-done = bf16[512,3,1024]{0,2,1:T(8,128)(2,1)} async-done(((bf16[128,3,1024]{0,2,1:T(8,128)(2,1)}), bf16[512,3,1024]{0,2,1:T(8,128)(2,1)}) %all-gather.6.cloned.1.call-update) | async-done | bytes 3145744 | tf_op jit(solution)/shard_map/all_gather | solution.py:107
  223.9 3.8 %reshape.8 = bf16[4,128,3,1024]{1,0,3,2:T(4,128)(2,1)S(1)} reshape(bf16[512,3,1024]{0,2,1:T(8,128)(2,1)} %all-gather.6.cloned.1.call-done) | data formatting | bytes 6291456 | tf_op jit(solution)/shard_map/all_gather | solution.py:107
  227.7 5.2 %reduce_sum.12 = bf16[128,3,1024]{0,2,1:T(8,128)(2,1)} reduce(bf16[4,128,3,1024]{1,0,3,2:T(4,128)(2,1)S(1)} %reshape.8, bf16[]{:T(256)} %constant.1.clone.1), dimensions={0}, to_apply=%region_1.0 | reduce | flops 1179648 | bytes 3932162 | tf_op jit(solution)/shard_map/reduce_sum | solution.py:107
  232.9 1.3 convert_multiply_fusion
  234.1 1.6 copy.12
  (17 shorter events, 0.0 us)
Async XLA Ops:
  7.2 33.7 %all-gather.4.cloned.1.call-start = ((), (), s32[]{:S(2)}) async-start(), calls=%async_computation.2 | async-start | bytes 3932160 | tf_op jit(solution)/shard_map/all_gather | solution.py:41
  7.9 61.9 %reduce-scatter.5.cloned.1.call-start = ((), (), s32[]{:S(2)}) async-start(), calls=%async_computation.3 | async-start | bytes 655360 | tf_op jit(solution)/shard_map/reduce_scatter | solution.py:97
  7.9 16.4 %collective-permute-start = (bf16[512,512]{1,0:T(8,128)(2,1)}, bf16[512,512]{1,0:T(8,128)(2,1)S(1)}, u32[]{:S(2)}, u32[]{:S(2)}) collective-permute-start(bf16[512,512]{1,0:T(8,128)(2,1)} %bitcast.59), channel_id=1, source_target_pairs={{0,4},{4,8},{8,12},{1,5},{5,9},{9,13},{2,6},{6,10},{10,14},{3,7},{... | collective-permute-start | bytes 1572872 | tf_op jit(solution)/shard_map/ppermute | solution.py:14
  20.3 24.4 %copy-start.3 = (bf16[512,512]{1,0:T(8,128)(2,1)}, bf16[512,512]{1,0:T(8,128)(2,1)S(1)}, u32[]{:S(2)}) copy-start(bf16[512,512]{1,0:T(8,128)(2,1)S(1)} %all_gather.15) | copy-start | bytes 1572868
  24.4 19.6 %collective-permute-start.1 = (bf16[512,512]{1,0:T(8,128)(2,1)S(1)}, bf16[512,512]{1,0:T(8,128)(2,1)S(1)}, u32[]{:S(2)}, u32[]{:S(2)}) collective-permute-start(bf16[512,512]{1,0:T(8,128)(2,1)S(1)} %collective-permute-done), channel_id=1, source_target_pairs={{0,4},{4,8},{8,12},{1,5},{5,9},{9,13},{2,6},{6,10},{10,14},{3,7},{... | collective-permute-start | bytes 1572872 | tf_op jit(solution)/shard_map/ppermute | solution.py:14
  40.8 2.4 copy-start
  43.9 1.0 copy-start.9
  45.9 0.8 copy-start.8
  45.9 3.6 %copy-start.4 = (bf16[512,512]{1,0:T(8,128)(2,1)}, bf16[512,512]{1,0:T(8,128)(2,1)S(1)}, u32[]{:S(2)}) copy-start(bf16[512,512]{1,0:T(8,128)(2,1)S(1)} %get-tuple-element.8) | copy-start | bytes 1572868
  45.9 3.6 %copy-start.6 = (bf16[512,512]{1,0:T(8,128)(2,1)}, bf16[512,512]{1,0:T(8,128)(2,1)S(1)}, u32[]{:S(2)}) copy-start(bf16[512,512]{1,0:T(8,128)(2,1)S(1)} %get-tuple-element.9) | copy-start | bytes 1572868
  45.9 2.1 copy-start.2
  48.0 62.5 %reduce-scatter.7.cloned.1.call-start = ((), (), s32[]{:S(2)}) async-start(), calls=%async_computation.6 | async-start | bytes 3932160
  53.7 99.2 %all-reduce.2.cloned.1.call-start = ((), (), s32[]{:S(2)}) async-start(), calls=%async_computation.4 | async-start | bytes 262144 | tf_op jit(solution)/shard_map/psum | solution.py:112
  69.8 154.2 %all-gather.6.cloned.1.call-start = ((), (), s32[]{:S(2)}) async-start(), calls=%async_computation.5 | async-start | bytes 3932160 | tf_op jit(solution)/shard_map/all_gather | solution.py:107
  112.8 36.4 %copy-start.1 = (bf16[512,3,1024]{2,0,1:T(8,128)(2,1)S(1)}, bf16[512,3,1024]{2,0,1:T(8,128)(2,1)}, u32[]{:S(2)}) copy-start(bf16[512,3,1024]{2,0,1:T(8,128)(2,1)} %all-gather.4.cloned.1.call-done) | copy-start | bytes 9437188
  112.9 36.4 %copy-start.5 = (bf16[512,512]{1,0:T(8,128)(2,1)S(1)}, bf16[512,512]{1,0:T(8,128)(2,1)}, u32[]{:S(2)}) copy-start(bf16[512,512]{1,0:T(8,128)(2,1)} %copy-done.4) | copy-start | bytes 1572868
  112.9 36.4 %copy-start.7 = (bf16[512,512]{1,0:T(8,128)(2,1)S(1)}, bf16[512,512]{1,0:T(8,128)(2,1)}, u32[]{:S(2)}) copy-start(bf16[512,512]{1,0:T(8,128)(2,1)} %copy-done.6) | copy-start | bytes 1572868
  114.3 30.8 %collective-permute-start.2 = (bf16[512,1024]{1,0:T(8,128)(2,1)S(1)}, bf16[512,1024]{1,0:T(8,128)(2,1)}, u32[]{:S(2)}, u32[]{:S(2)}) collective-permute-start(bf16[512,1024]{1,0:T(8,128)(2,1)S(1)} %pad_maximum_fusion.1), channel_id=1, source_target_pairs={{4,0},{8,4},{12,8},{5,1},{9,5},{13,9},{6,2},{10,6},{14,10},{7,3},{... | collective-permute-start | bytes 3145736 | tf_op jit(solution)/shard_map/ppermute | solution.py:14
  145.1 47.9 %collective-permute-start.3 = (bf16[512,1024]{1,0:T(8,128)(2,1)}, bf16[512,1024]{1,0:T(8,128)(2,1)}, u32[]{:S(2)}, u32[]{:S(2)}) collective-permute-start(bf16[512,1024]{1,0:T(8,128)(2,1)} %collective-permute-done.2), channel_id=1, source_target_pairs={{4,0},{8,4},{12,8},{5,1},{9,5},{13,9},{6,2},{10,6},{14,10},{7,3},{... | collective-permute-start | bytes 3145736 | tf_op jit(solution)/shard_map/ppermute | solution.py:14
Sparse Core Ops, SparseCore 0:
  9.6 31.2 all-gather.3
  48.1 21.6 reduce-scatter.4
  72.5 37.9 reduce-scatter.6
  112.6 35.0 all-reduce.1
  149.2 74.7 all-gather.5
